TPU v7x, 512 devices: a whole 4x4x16 slice. The times are simulated.
512 devices in a mesh: dom: 64 (over x, z), head: 8 (over y, core).
Axes of the slice: x: 4, y: 4, z: 16, core: 2. Of those that a mesh axis runs over, the one named last changes fastest.
Arguments:
- node_feats: bfloat16 [65536, 512], P(('dom', 'head')), may hold values from -6 to 6
- norm_gain: float32 [512], replicated, may hold values from 0.25 to 1.75
- w_qkv: bfloat16 [512, 1536], P(None, 'head'), may hold values from -1 to 1
- w_out: bfloat16 [512, 512], replicated, may hold values from -0.25 to 0.25
- rand_feat: float32 [8, 64, 256], P('head'), may hold values from -6 to 6
- temper: float32 [8], P('head'), may hold values from 1 to 6
- edge_src: int32 [512, 6], P('dom'), may hold values from 0 to 511, as said below
- edge_count: int32 [512], P('dom'), may hold values from 1 to 6, as said below
- block_fill: int32 [512], replicated, may hold values from 32 to 128, as said below
Outputs:
- update: bfloat16 [65536, 512], P(('dom', 'head'))
Inputs may be any that keep to these rules, and one draw needn't show every extreme that they name: `edge_src`: destination block b lies in partition p = b // 8; each of its source blocks lies in partition p - 1, p or p + 1; slot 0 holds b itself, and slots at or beyond edge_count[b] hold b. `edge_count`: every block of some partition uses all 6 slots. `block_fill`: block 0 is full.
All inputs are finite; a program needn't handle non-finite values.
Results may differ from a plain program's by a relative error of at most 0.012.
The roundings to bfloat16 on the way count: a program that leaves them out, or rounds other values in their place, can miss the bound.
Values may be sent and summed in bfloat16 or wider, within the bound.
A program may use at most 64 MiB of HBM per device.

v0:
```python
import math
import jax
import jax.numpy as jnp
from jax import lax
from jax.sharding import PartitionSpec as P

BLK = 128


def padded(block, sides, width):
    for axis, dim in sides:
        count = lax.axis_size(axis)
        forward = [(i, i + 1) for i in range(count - 1)]
        backward = [(target, source) for source, target in forward]
        low = lax.ppermute(
            lax.slice_in_dim(block, block.shape[dim] - width, None, axis=dim), axis, forward
        )
        high = lax.ppermute(lax.slice_in_dim(block, 0, width, axis=dim), axis, backward)
        block = jnp.concatenate([low, block, high], axis=dim)
    return block


def layer_norm(rows, gain):
    widened = rows.astype(jnp.float32)
    centred = widened - jnp.mean(widened, axis=-1, keepdims=True)
    spread = jnp.mean(centred * centred, axis=-1, keepdims=True)
    return (centred * lax.rsqrt(spread + 1e-05) * gain).astype(jnp.bfloat16)


def features(rows, directions, temper):
    head_dim = rows.shape[-1]
    scaled = rows.astype(jnp.float32) * (jnp.sqrt(temper)[None, :, None] * head_dim ** (-0.25))
    lifted = jnp.einsum("nhd,hdm->nhm", scaled, directions, precision=lax.Precision.HIGHEST)
    return jnp.exp(
        lifted - 0.5 * jnp.sum(scaled * scaled, axis=-1, keepdims=True)
    ) * directions.shape[2] ** (-0.5)


def shards(
    node_feats, norm_gain, w_qkv, w_out, rand_feat, temper, edge_src, edge_count, block_fill
):
    groups = lax.axis_size("head")
    heads_here = rand_feat.shape[0]
    head_dim = rand_feat.shape[1]
    part_rows = node_feats.shape[0] * groups
    blocks = part_rows // BLK
    slots = edge_src.shape[1]
    domain = lax.axis_index("dom")
    normed = layer_norm(node_feats, norm_gain)
    qkv = jnp.dot(
        lax.all_gather(normed, "head", axis=0, tiled=True),
        w_qkv,
        preferred_element_type=jnp.float32,
    ).astype(jnp.bfloat16)
    split = qkv.reshape(part_rows, heads_here, 3, head_dim)
    queries = split[:, :, 0]
    own_fill = lax.dynamic_slice_in_dim(block_fill, domain * blocks, blocks)
    lanes = lax.broadcasted_iota(jnp.int32, (blocks, BLK), 1)
    valid = (lanes < own_fill[:, None]).astype(jnp.float32).reshape(part_rows)
    phi_keys = features(split[:, :, 1], rand_feat, temper) * valid[:, None, None]
    partial_sum = jnp.einsum(
        "nhm,nhe->hme",
        phi_keys,
        split[:, :, 2].astype(jnp.float32),
        precision=lax.Precision.HIGHEST,
    )
    kernel_sum, key_total = lax.psum((partial_sum, jnp.sum(phi_keys, axis=0)), "dom")
    pairs = split[:, :, 1:].reshape(part_rows, heads_here * 2 * head_dim)
    widened = padded(pairs, (("dom", 0),), part_rows)
    kv_blocks = widened.reshape(3 * blocks, BLK, heads_here, 2, head_dim)
    key_blocks = kv_blocks[:, :, :, 0]
    value_blocks = kv_blocks[:, :, :, 1]
    local_src = edge_src - (domain - 1) * blocks
    scale = head_dim ** (-0.5)
    per_step = math.gcd(blocks, max(1, 8 // heads_here))
    turns = blocks // per_step
    width = slots * BLK
    q_steps = queries.reshape(turns, per_step, BLK, heads_here, head_dim)
    src_steps = local_src.reshape(turns, per_step, slots)
    id_steps = edge_src.reshape(turns, per_step, slots)
    count_steps = edge_count.reshape(turns, per_step)

    def attend_all(packed):
        q_part, src_part, id_part, count_part = packed
        keys = jnp.take(key_blocks, src_part, axis=0).reshape(per_step, width, heads_here, head_dim)
        values = jnp.take(value_blocks, src_part, axis=0).reshape(
            per_step, width, heads_here, head_dim
        )
        fills = jnp.take(block_fill, id_part)
        slot_ids = lax.broadcasted_iota(jnp.int32, (per_step, slots, BLK), 1)
        lane_ids = lax.broadcasted_iota(jnp.int32, (per_step, slots, BLK), 2)
        allowed = ((lane_ids < fills[:, :, None]) & (slot_ids < count_part[:, None, None])).reshape(
            per_step, width
        )
        scores = (
            jnp.einsum("bqhd,bkhd->bhqk", q_part, keys, preferred_element_type=jnp.float32) * scale
        )
        scores = jnp.where(allowed[:, None, None, :], scores, -1e30)
        row_max = jnp.max(scores, axis=3, keepdims=True)
        weights = jnp.exp(scores - row_max)
        total = jnp.sum(weights, axis=3)
        accum = jnp.einsum(
            "bhqk,bkhd->bqhd",
            weights.astype(jnp.bfloat16),
            values,
            preferred_element_type=jnp.float32,
        )
        return accum / jnp.transpose(total, (0, 2, 1))[..., None]

    local = lax.map(attend_all, (q_steps, src_steps, id_steps, count_steps))
    local = local.reshape(part_rows, heads_here, head_dim)
    phi_queries = features(queries, rand_feat, temper)
    numer = jnp.einsum("nhm,hme->nhe", phi_queries, kernel_sum, precision=lax.Precision.HIGHEST)
    denom = jnp.einsum("nhm,hm->nh", phi_queries, key_total, precision=lax.Precision.HIGHEST)
    mixed = (
        (local + numer / denom[..., None])
        .astype(jnp.bfloat16)
        .reshape(part_rows, heads_here * head_dim)
    )
    returned = lax.all_to_all(mixed, "head", split_axis=0, concat_axis=1, tiled=True)
    return jnp.dot(returned, w_out, preferred_element_type=jnp.float32).astype(jnp.bfloat16)


def solution(mesh):
    return jax.shard_map(
        shards,
        mesh=mesh,
        in_specs=(
            P(("dom", "head"), None),
            P(),
            P(None, "head"),
            P(),
            P("head", None, None),
            P("head"),
            P("dom", None),
            P("dom"),
            P(),
        ),
        out_specs=P(("dom", "head"), None),
        check_vma=False,
    )
```

profile of v0, /device:TPU:1, one launch (start us, length us, event | category | flops | bytes accessed | tf_op | source)
XLA Modules:
  0.0 337.9 jit_solution(1613953993842794324)
XLA Ops:
  6.6 1.1 convert_reduce_fusion
  7.7 1.1 fusion.31
  8.8 1.7 fusion.33
  10.6 1.3 compare_and_fusion
  11.9 0.7 compare_select_fusion.1
  12.7 0.8 gather_fusion
  14.6 33.0 %all-gather.2.cloned.1.call-done = bf16[1024,512]{1,0:T(8,128)(2,1)} async-done(((bf16[128,512]{1,0:T(8,128)(2,1)}), bf16[1024,512]{1,0:T(8,128)(2,1)}) %all-gather.2.cloned.1.call-update) | async-done | bytes 1048592 | tf_op jit(solution)/shard_map/all_gather | solution.py:51
  47.6 1.7 convolution_convert_fusion
  49.4 3.0 collective-permute-start
  52.4 1.3 collective-permute-start.1
  53.9 1.3 fusion.48
  55.1 1.1 fusion.27
  56.2 1.1 fusion.12
  57.4 0.7 copy.30
  58.1 117.4 %psum.15 = f32[256]{0:T(256)S(1)} all-reduce(f32[256]{0:T(256)S(1)} %get-tuple-element.43), channel_id=1, replica_groups=mesh['dom'=64,'head'=8] {'dom'}, use_global_device_ids=true, to_apply=%region_8.10 | all-reduce | flops 256 | bytes 2048 | tf_op jit(solution)/shard_map/psum | solution.py:67
  175.5 1.0 fusion.49
  176.8 0.2 copy_bitcast_fusion
  177.0 0.7 gather_fusion.1
  177.7 0.7 gather_fusion.2
  178.4 1.8 broadcast_select_fusion
  180.2 0.6 copy.22
  180.7 0.9 reshape.266
  181.6 1.7 copy.19
  183.3 1.8 reshape.264
  185.1 0.7 fusion
  185.8 0.9 fusion.1
  186.8 1.0 fusion.24
  187.7 0.2 copy.24
  187.9 120.0 %all-reduce.2.cloned.1.call-done = f32[256,64]{0,1:T(8,128)} async-done(((f32[256,64]{0,1:T(8,128)}), f32[256,64]{0,1:T(8,128)}) %all-reduce.2.cloned.1.call-update) | async-done | bytes 65552 | tf_op jit(solution)/shard_map/psum | solution.py:67
  307.9 2.0 fusion.20
  309.9 20.3 %all_to_all.19 = bf16[8,128,64]{1,2,0:T(8,128)(2,1)S(1)} all-to-all(bf16[8,128,64]{1,2,0:T(8,128)(2,1)S(1)} %copy.26), channel_id=1, replica_groups=mesh['dom'=64,'head'=8] {'head'}, dimensions={0} | all-to-all | bytes 262144 | tf_op jit(solution)/shard_map/all_to_all | solution.py:120
  330.2 0.9 convolution_convert_fusion.1
  (45 shorter events, 1.2 us)
Async XLA Ops:
  6.5 323.6 %copy-start = (bf16[512,512]{1,0:T(8,128)(2,1)S(1)}, bf16[512,512]{1,0:T(8,128)(2,1)}, u32[]{:S(2)}) copy-start(bf16[512,512]{1,0:T(8,128)(2,1)} %param.14) | copy-start | bytes 1572868
  6.5 7.1 %copy-start.6 = (s32[8,6]{1,0:T(8,128)S(1)}, s32[8,6]{1,0:T(8,128)}, u32[]{:S(2)}) copy-start(s32[8,6]{1,0:T(8,128)} %param.17) | copy-start | bytes 580
  6.5 6.2 %copy-start.1 = (s32[512]{0:T(512)S(1)}, s32[512]{0:T(512)}, u32[]{:S(2)}) copy-start(s32[512]{0:T(512)} %param.19) | copy-start | bytes 6148
  6.5 8.0 %copy-start.7 = (s32[8]{0:T(128)S(1)}, s32[8]{0:T(128)}, u32[]{:S(2)}) copy-start(s32[8]{0:T(128)} %param.18) | copy-start | bytes 100
  6.5 41.1 %copy-start.5 = (bf16[512,192]{0,1:T(8,128)(2,1)S(1)}, bf16[512,192]{0,1:T(8,128)(2,1)}, u32[]{:S(2)}) copy-start(bf16[512,192]{0,1:T(8,128)(2,1)} %param.13) | copy-start | bytes 589828
  6.5 41.1 %all-gather.2.cloned.1.call-start = ((), (), s32[]{:S(2)}) async-start(), calls=%async_computation.1 | async-start | bytes 1179648 | tf_op jit(solution)/shard_map/all_gather | solution.py:51
  10.5 297.3 %all-reduce.2.cloned.1.call-start = ((), (), s32[]{:S(2)}) async-start(), calls=%async_computation.2 | async-start | bytes 131072 | tf_op jit(solution)/shard_map/psum | solution.py:67
  12.7 41.1 %copy-start.4 = (f32[1,64,256]{2,1,0:T(8,128)S(1)}, f32[1,64,256]{2,1,0:T(8,128)}, u32[]{:S(2)}) copy-start(f32[1,64,256]{2,1,0:T(8,128)} %param.15) | copy-start | bytes 196612
  49.4 127.1 %collective-permute-start = (bf16[1024,128]{0,1:T(8,128)(2,1)S(1)}, bf16[1024,128]{0,1:T(8,128)(2,1)S(1)}, u32[]{:S(2)}, u32[]{:S(2)}) collective-permute-start(bf16[1024,128]{0,1:T(8,128)(2,1)S(1)} %bitcast.148), channel_id=1, source_target_pairs={{0,8},{8,16},{16,24},{24,32},{32,40},{40,48},{48,56},{56,64},{64,7... | collective-permute-start | bytes 786440 | tf_op jit(solution)/shard_map/ppermute | solution.py:15
  52.4 124.1 %collective-permute-start.1 = (bf16[1024,128]{0,1:T(8,128)(2,1)S(1)}, bf16[1024,128]{0,1:T(8,128)(2,1)S(1)}, u32[]{:S(2)}, u32[]{:S(2)}) collective-permute-start(bf16[1024,128]{0,1:T(8,128)(2,1)S(1)} %bitcast.149), channel_id=1, source_target_pairs={{8,0},{16,8},{24,16},{32,24},{40,32},{48,40},{56,48},{64,56},{72,6... | collective-permute-start | bytes 786440 | tf_op jit(solution)/shard_map/ppermute | solution.py:18
  180.7 4.4 %copy-start.3 = (bf16[8,8,8,128]{3,2,1,0:T(8,128)(2,1)S(1)}, bf16[8,8,8,128]{3,2,1,0:T(8,128)(2,1)}, u32[]{:S(2)}) copy-start(bf16[8,8,8,128]{3,2,1,0:T(8,128)(2,1)} %copy.30) | copy-start | bytes 393220
  185.1 1.6 copy-start.2
Sparse Core Ops, SparseCore 0:
  10.6 36.9 all-gather.1
  58.2 249.6 all-reduce.1
where the time goes:
time: 338 us
  waiting for transfers between devices  153 us (45%)
  blocking collectives  138 us (41%)
  between operations  14.4 us (4%)
  matrix products  10.7 us (3%)
  local copies, waits for them, and re-layouts  8.88 us (3%)
  other arithmetic  8.83 us (3%)
  starting transfers between devices  4.4 us (1%)
    psum x1, waiting for transfers between devices, shards(): lax.psum((partial_sum, jnp.sum(phi_keys, axis=0)), 'dom')  120 us
    psum x1, blocking collectives, shards(): lax.psum((partial_sum, jnp.sum(phi_keys, axis=0)), 'dom')  117 us
    all_gather x1, waiting for transfers between devices, shards(): lax.all_gather(normed, 'head', axis=0, tiled=True)  33 us
    all_to_all x1, blocking collectives, shards(): lax.all_to_all(mixed, 'head', split_axis=0, concat_axis=1, tiled=True)  20.3 us
  transfers between devices with their start and end apart: 4, of which 2 were waited for; matrix products, arithmetic and copies ran while one was open for 6% of the time, Pallas kernels for 0%

commit v1 on v0

--- a/solution.py
+++ b/solution.py
@@ -5,6 +5,27 @@
 from jax.sharding import PartitionSpec as P
 
 BLK = 128
+
+
+def ring_gather(x, axis, dim):
+    size, position, width = (lax.axis_size(axis), lax.axis_index(axis), x.shape[dim])
+    right = [(i, (i + 1) % size) for i in range(size)]
+    left = [(i, (i - 1) % size) for i in range(size)]
+    out = jnp.zeros((*x.shape[:dim], size * width, *x.shape[dim + 1 :]), x.dtype)
+    out = lax.dynamic_update_slice_in_dim(out, x, position * width, axis=dim)
+    from_left = from_right = x
+    half = size // 2
+    for turn in range(1, half + 1):
+        from_left = lax.ppermute(from_left, axis, right)
+        out = lax.dynamic_update_slice_in_dim(
+            out, from_left, (position - turn) % size * width, axis=dim
+        )
+        if turn < size - half:
+            from_right = lax.ppermute(from_right, axis, left)
+            out = lax.dynamic_update_slice_in_dim(
+                out, from_right, (position + turn) % size * width, axis=dim
+            )
+    return out
 
 
 def padded(block, sides, width):
@@ -47,11 +68,9 @@
     slots = edge_src.shape[1]
     domain = lax.axis_index("dom")
     normed = layer_norm(node_feats, norm_gain)
-    qkv = jnp.dot(
-        lax.all_gather(normed, "head", axis=0, tiled=True),
-        w_qkv,
-        preferred_element_type=jnp.float32,
-    ).astype(jnp.bfloat16)
+    qkv = jnp.dot(ring_gather(normed, "head", 0), w_qkv, preferred_element_type=jnp.float32).astype(
+        jnp.bfloat16
+    )
     split = qkv.reshape(part_rows, heads_here, 3, head_dim)
     queries = split[:, :, 0]
     own_fill = lax.dynamic_slice_in_dim(block_fill, domain * blocks, blocks)

time: 338 us -> 327 us (0.967)
  waiting for transfers between devices: 153 us -> 128 us
  starting transfers between devices: 4.4 us -> 17.2 us
    all_gather x1 -> x0, waiting for transfers between devices: 33 us -> none  [shards(): lax.all_gather(normed, 'head', axis=0, tiled=True)]
    ppermute x0 -> x7, starting transfers between devices: none -> 14.6 us  [the longest x3 11.3 us: ring_gather(): from_right = lax.ppermute(from_right, axis, left)]
    ppermute x0 -> x7, waiting for transfers between devices: none -> 7.16 us  [the longest x4 7 us: ring_gather(): from_left = lax.ppermute(from_left, axis, right)]
  transfers between devices with their start and end apart: 4 -> 10, of which waited for: 2 -> 5; matrix products, arithmetic and copies ran while one was open for 6% -> 6% of each run, Pallas kernels for 0% -> 0%
where the time goes in v1:
time: 327 us; the launch traced here: 326 us
  blocking collectives  140 us (43%)
  waiting for transfers between devices  128 us (39%)
  starting transfers between devices  17.2 us (5%)
  between operations  14.5 us (4%)
  matrix products  9.48 us (3%)
  local copies, waits for them, and re-layouts  9.05 us (3%)
  other arithmetic  8.08 us (2%)
    psum x1, waiting for transfers between devices, shards(): lax.psum((partial_sum, jnp.sum(phi_keys, axis=0)), 'dom')  121 us
    psum x1, blocking collectives, shards(): lax.psum((partial_sum, jnp.sum(phi_keys, axis=0)), 'dom')  120 us
    all_to_all x1, blocking collectives, shards(): lax.all_to_all(mixed, 'head', split_axis=0, concat_axis=1, tiled=True)  20.3 us
    ppermute x3, starting transfers between devices, ring_gather(): from_right = lax.ppermute(from_right, axis, left)  11.3 us
    ppermute x4, waiting for transfers between devices, ring_gather(): from_left = lax.ppermute(from_left, axis, right)  7 us
  transfers between devices with their start and end apart: 10, of which 5 were waited for; matrix products, arithmetic and copies ran while one was open for 6% of the time, Pallas kernels for 0%

profile of v1, /device:TPU:1, one launch (start us, length us, event | category | flops | bytes accessed | tf_op | source)
XLA Modules:
  0.0 326.2 jit_solution(827262008892163832)
XLA Ops:
  6.6 1.1 convert_reduce_fusion
  7.7 1.1 fusion.31
  8.8 1.0 constant_dynamic-update-slice_fusion.7
  9.9 2.7 collective-permute-start
  12.6 4.2 %collective-permute-start.1 = (bf16[128,512]{1,0:T(8,128)(2,1)S(1)}, bf16[128,512]{1,0:T(8,128)(2,1)S(1)}, u32[]{:S(2)}, u32[]{:S(2)}) collective-permute-start(bf16[128,512]{1,0:T(8,128)(2,1)S(1)} %get-tuple-element.36), channel_id=1, source_target_pairs={{0,7},{1,0},{2,1},{3,2},{4,3},{5,4},{6,5},{7,6},{8,15},{9,8},{10,9... | collective-permute-start | bytes 393224 | tf_op jit(solution)/shard_map/ppermute | solution.py:24
  17.5 1.2 compare_and_fusion
  18.8 0.8 gather_fusion
  21.0 2.9 collective-permute-start.3
  24.0 0.8 collective-permute-done.2
  25.4 4.1 %collective-permute-start.5 = (bf16[128,512]{1,0:T(8,128)(2,1)S(1)}, bf16[128,512]{1,0:T(8,128)(2,1)S(1)}, u32[]{:S(2)}, u32[]{:S(2)}) collective-permute-start(bf16[128,512]{1,0:T(8,128)(2,1)S(1)} %collective-permute-done.3), channel_id=1, source_target_pairs={{0,7},{1,0},{2,1},{3,2},{4,3},{5,4},{6,5},{7,6},{8,15},{9,8},{10,9... | collective-permute-start | bytes 393224 | tf_op jit(solution)/shard_map/ppermute | solution.py:24
  29.5 0.8 collective-permute-done.4
  30.5 5.4 %collective-permute-done.6 = bf16[128,512]{1,0:T(8,128)(2,1)S(1)} collective-permute-done((bf16[128,512]{1,0:T(8,128)(2,1)S(1)}, bf16[128,512]{1,0:T(8,128)(2,1)S(1)}, u32[]{:S(2)}, u32[]{:S(2)}) %collective-permute-start.6) | collective-permute-done | bytes 131104 | tf_op jit(solution)/shard_map/ppermute | solution.py:19
  36.5 1.3 collective-permute-start.7
  37.8 1.3 collective-permute-start.8
  39.3 1.2 fusion.49
  40.5 1.1 fusion.27
  41.6 1.1 fusion.12
  43.5 119.8 %psum.15 = f32[256]{0:T(256)S(1)} all-reduce(f32[256]{0:T(256)S(1)} %get-tuple-element.45), channel_id=1, replica_groups=mesh['dom'=64,'head'=8] {'dom'}, use_global_device_ids=true, to_apply=%region_8.10 | all-reduce | flops 256 | bytes 2048 | tf_op jit(solution)/shard_map/psum | solution.py:86
  163.2 1.0 fusion.50
  164.7 0.7 gather_fusion.1
  165.4 0.7 gather_fusion.2
  166.1 1.7 broadcast_select_fusion
  168.4 0.9 reshape.266
  169.3 1.7 copy.19
  171.0 1.8 reshape.264
  172.8 0.7 fusion
  173.5 0.9 fusion.1
  174.5 1.0 fusion.24
  175.6 120.5 %all-reduce.2.cloned.1.call-done = f32[256,64]{0,1:T(8,128)} async-done(((f32[256,64]{0,1:T(8,128)}), f32[256,64]{0,1:T(8,128)}) %all-reduce.2.cloned.1.call-update) | async-done | bytes 65552 | tf_op jit(solution)/shard_map/psum | solution.py:86
  296.1 2.0 fusion.20
  298.2 20.3 %all_to_all.19 = bf16[8,128,64]{1,2,0:T(8,128)(2,1)S(1)} all-to-all(bf16[8,128,64]{1,2,0:T(8,128)(2,1)S(1)} %copy.26), channel_id=1, replica_groups=mesh['dom'=64,'head'=8] {'head'}, dimensions={0} | all-to-all | bytes 262144 | tf_op jit(solution)/shard_map/all_to_all | solution.py:139
  318.5 0.9 convolution_convert_fusion.1
  (64 shorter events, 4.9 us)
Async XLA Ops:
  6.5 311.9 %copy-start = (bf16[512,512]{1,0:T(8,128)(2,1)S(1)}, bf16[512,512]{1,0:T(8,128)(2,1)}, u32[]{:S(2)}) copy-start(bf16[512,512]{1,0:T(8,128)(2,1)} %param.14) | copy-start | bytes 1572868
  6.5 13.2 %copy-start.6 = (s32[8,6]{1,0:T(8,128)S(1)}, s32[8,6]{1,0:T(8,128)}, u32[]{:S(2)}) copy-start(s32[8,6]{1,0:T(8,128)} %param.17) | copy-start | bytes 580
  6.5 12.3 %copy-start.1 = (s32[512]{0:T(512)S(1)}, s32[512]{0:T(512)}, u32[]{:S(2)}) copy-start(s32[512]{0:T(512)} %param.19) | copy-start | bytes 6148
  6.5 13.4 %copy-start.7 = (s32[8]{0:T(128)S(1)}, s32[8]{0:T(128)}, u32[]{:S(2)}) copy-start(s32[8]{0:T(128)} %param.18) | copy-start | bytes 100
  6.5 289.6 %all-reduce.2.cloned.1.call-start = ((), (), s32[]{:S(2)}) async-start(), calls=%async_computation.1 | async-start | bytes 131072 | tf_op jit(solution)/shard_map/psum | solution.py:86
  9.9 11.0 %collective-permute-start = (bf16[128,512]{1,0:T(8,128)(2,1)S(1)}, bf16[128,512]{1,0:T(8,128)(2,1)S(1)}, u32[]{:S(2)}, u32[]{:S(2)}) collective-permute-start(bf16[128,512]{1,0:T(8,128)(2,1)S(1)} %get-tuple-element.36), channel_id=1, source_target_pairs={{0,1},{1,2},{2,3},{3,4},{4,5},{5,6},{6,7},{7,0},{8,9},{9,10},{10,1... | collective-permute-start | bytes 393224 | tf_op jit(solution)/shard_map/ppermute | solution.py:19
  12.6 8.4 %collective-permute-start.1 = (bf16[128,512]{1,0:T(8,128)(2,1)S(1)}, bf16[128,512]{1,0:T(8,128)(2,1)S(1)}, u32[]{:S(2)}, u32[]{:S(2)}) collective-permute-start(bf16[128,512]{1,0:T(8,128)(2,1)S(1)} %get-tuple-element.36), channel_id=1, source_target_pairs={{0,7},{1,0},{2,1},{3,2},{4,3},{5,4},{6,5},{7,6},{8,15},{9,8},{10,9... | collective-permute-start | bytes 393224 | tf_op jit(solution)/shard_map/ppermute | solution.py:24
  18.8 17.1 %copy-start.5 = (bf16[512,192]{0,1:T(8,128)(2,1)S(1)}, bf16[512,192]{0,1:T(8,128)(2,1)}, u32[]{:S(2)}) copy-start(bf16[512,192]{0,1:T(8,128)(2,1)} %param.13) | copy-start | bytes 589828
  19.6 19.6 %copy-start.4 = (f32[1,64,256]{2,1,0:T(8,128)S(1)}, f32[1,64,256]{2,1,0:T(8,128)}, u32[]{:S(2)}) copy-start(f32[1,64,256]{2,1,0:T(8,128)} %param.15) | copy-start | bytes 196612
  20.9 3.8 %collective-permute-start.2 = (bf16[128,512]{1,0:T(8,128)(2,1)S(1)}, bf16[128,512]{1,0:T(8,128)(2,1)S(1)}, u32[]{:S(2)}, u32[]{:S(2)}) collective-permute-start(bf16[128,512]{1,0:T(8,128)(2,1)S(1)} %collective-permute-done), channel_id=1, source_target_pairs={{0,1},{1,2},{2,3},{3,4},{4,5},{5,6},{6,7},{7,0},{8,9},{9,10},{10,1... | collective-permute-start | bytes 393224 | tf_op jit(solution)/shard_map/ppermute | solution.py:19
  21.0 4.4 %collective-permute-start.3 = (bf16[128,512]{1,0:T(8,128)(2,1)S(1)}, bf16[128,512]{1,0:T(8,128)(2,1)S(1)}, u32[]{:S(2)}, u32[]{:S(2)}) collective-permute-start(bf16[128,512]{1,0:T(8,128)(2,1)S(1)} %collective-permute-done.1), channel_id=1, source_target_pairs={{0,7},{1,0},{2,1},{3,2},{4,3},{5,4},{6,5},{7,6},{8,15},{9,8},{10,9... | collective-permute-start | bytes 393224 | tf_op jit(solution)/shard_map/ppermute | solution.py:24
  24.7 5.6 %collective-permute-start.4 = (bf16[128,512]{1,0:T(8,128)(2,1)S(1)}, bf16[128,512]{1,0:T(8,128)(2,1)S(1)}, u32[]{:S(2)}, u32[]{:S(2)}) collective-permute-start(bf16[128,512]{1,0:T(8,128)(2,1)S(1)} %collective-permute-done.2), channel_id=1, source_target_pairs={{0,1},{1,2},{2,3},{3,4},{4,5},{5,6},{6,7},{7,0},{8,9},{9,10},{10,1... | collective-permute-start | bytes 393224 | tf_op jit(solution)/shard_map/ppermute | solution.py:19
  25.4 5.1 %collective-permute-start.5 = (bf16[128,512]{1,0:T(8,128)(2,1)S(1)}, bf16[128,512]{1,0:T(8,128)(2,1)S(1)}, u32[]{:S(2)}, u32[]{:S(2)}) collective-permute-start(bf16[128,512]{1,0:T(8,128)(2,1)S(1)} %collective-permute-done.3), channel_id=1, source_target_pairs={{0,7},{1,0},{2,1},{3,2},{4,3},{5,4},{6,5},{7,6},{8,15},{9,8},{10,9... | collective-permute-start | bytes 393224 | tf_op jit(solution)/shard_map/ppermute | solution.py:24
  30.3 5.6 %collective-permute-start.6 = (bf16[128,512]{1,0:T(8,128)(2,1)S(1)}, bf16[128,512]{1,0:T(8,128)(2,1)S(1)}, u32[]{:S(2)}, u32[]{:S(2)}) collective-permute-start(bf16[128,512]{1,0:T(8,128)(2,1)S(1)} %collective-permute-done.4), channel_id=1, source_target_pairs={{0,1},{1,2},{2,3},{3,4},{4,5},{5,6},{6,7},{7,0},{8,9},{9,10},{10,1... | collective-permute-start | bytes 393224 | tf_op jit(solution)/shard_map/ppermute | solution.py:19
  36.5 127.7 %collective-permute-start.7 = (bf16[1024,128]{0,1:T(8,128)(2,1)S(1)}, bf16[1024,128]{0,1:T(8,128)(2,1)S(1)}, u32[]{:S(2)}, u32[]{:S(2)}) collective-permute-start(bf16[1024,128]{0,1:T(8,128)(2,1)S(1)} %bitcast.148), channel_id=1, source_target_pairs={{0,8},{8,16},{16,24},{24,32},{32,40},{40,48},{48,56},{56,64},{64,7... | collective-permute-start | bytes 786440 | tf_op jit(solution)/shard_map/ppermute | solution.py:36
  37.8 126.4 %collective-permute-start.8 = (bf16[1024,128]{0,1:T(8,128)(2,1)S(1)}, bf16[1024,128]{0,1:T(8,128)(2,1)S(1)}, u32[]{:S(2)}, u32[]{:S(2)}) collective-permute-start(bf16[1024,128]{0,1:T(8,128)(2,1)S(1)} %bitcast.149), channel_id=1, source_target_pairs={{8,0},{16,8},{24,16},{32,24},{40,32},{48,40},{56,48},{64,56},{72,6... | collective-permute-start | bytes 786440 | tf_op jit(solution)/shard_map/ppermute | solution.py:39
  168.4 4.4 %copy-start.3 = (bf16[8,8,8,128]{3,2,1,0:T(8,128)(2,1)S(1)}, bf16[8,8,8,128]{3,2,1,0:T(8,128)(2,1)}, u32[]{:S(2)}) copy-start(bf16[8,8,8,128]{3,2,1,0:T(8,128)(2,1)} %copy.30) | copy-start | bytes 393220
  172.8 1.6 copy-start.2
Sparse Core Ops, SparseCore 0:
  43.6 252.5 all-reduce.1
